TPU v7x, 32 devices: a whole 2x2x4 slice. The times are simulated.
32 devices in a mesh: node: 16 (over z, x, core), local: 2 (over y).
Axes of the slice: x: 2, y: 2, z: 4, core: 2. Of those that a mesh axis runs over, the one named last changes fastest.
Arguments:
- master_weight: bfloat16 [64, 128, 2048], P(None, 'node', 'local'), may hold values from -6 to 6
- first_moment: float32 [64, 128, 2048], P(None, 'node', 'local'), may hold values from -6 to 6
- second_moment: float32 [64, 128, 2048], P(None, 'node', 'local'), may hold values from 0.25 to 4
- features: bfloat16 [96, 2, 128, 128], P('node', 'local'), may hold values from -6 to 6
- grad_out: bfloat16 [96, 2, 128, 2048], P('node', 'local'), may hold values from -0.375 to 0.375
- old_place: int32 [80], replicated, may hold values from 0 to 95, as said below
- new_place: int32 [80], replicated, may hold values from 0 to 95, as said below
- old_owner: int32 [16], replicated, may hold values from 0 to 63
- new_owner: int32 [16], replicated, may hold values from 0 to 63
Outputs:
- slot_weight: bfloat16 [96, 128, 2048], P('node', None, 'local')
- slot_first: float32 [96, 128, 2048], P('node', None, 'local')
- slot_second: float32 [96, 128, 2048], P('node', None, 'local')
Inputs may be any that keep to these rules, and one draw needn't show every extreme that they name: `old_place`: 80 distinct positions; position p belongs to node p // 6; in every draw some node has all 6 of its positions taken. `new_place`: 80 distinct positions; position p belongs to node p // 6; in every draw some node has all 6 of its positions taken.
All inputs are finite; a program needn't handle non-finite values.
Results may differ from a plain program's by a relative error of at most 0.0044.
Values may be sent and summed in bfloat16 or wider, within the bound.
No kernel may reach another device: no remote copies, remote signals or barrier semaphores. Data moves between devices by JAX's collectives and lax.ppermute only.
A program may use at most 64 MiB of HBM per device.

v0:
```python
import jax
import jax.numpy as jnp
from jax import lax
from jax.sharding import PartitionSpec as P

BETA_FIRST = 0.9
BETA_SECOND = 0.95
LEARNING_RATE = 0.1
DECAY_RATE = 0.1
EPSILON = 1e-08
CORRECT_FIRST = 1.0 - 0.9**10
CORRECT_SECOND = 1.0 - 0.95**10


def one_hot(values, length):
    return (values[:, None] == jnp.arange(length, dtype=jnp.int32)[None, :]).astype(jnp.float32)


def local(
    master_weight,
    first_moment,
    second_moment,
    features,
    grad_out,
    old_place,
    new_place,
    old_owner,
    new_owner,
):
    node_count = lax.axis_size("node")
    capacity = features.shape[0]
    experts = master_weight.shape[0]
    block_rows = master_weight.shape[1]
    columns = master_weight.shape[2]
    hidden_width = grad_out.shape[3]
    positions = node_count * capacity
    primaries = jnp.arange(experts, dtype=jnp.int32)
    old_expert = jnp.concatenate([primaries, old_owner])
    new_expert = jnp.concatenate([primaries, new_owner])
    slot_grad = jnp.einsum("cltr,cltf->crf", features, grad_out, preferred_element_type=jnp.float32)
    collect = jnp.dot(
        one_hot(old_expert, experts).T,
        one_hot(old_place, positions),
        precision=lax.Precision.HIGHEST,
    )
    collect = collect.reshape(experts, node_count, capacity)
    blocks = lax.all_to_all(
        slot_grad.reshape(capacity, node_count, block_rows, hidden_width).astype(jnp.bfloat16),
        "node",
        split_axis=1,
        concat_axis=1,
        tiled=True,
    ).astype(jnp.float32)
    summed = jnp.einsum(
        "ekc,ckx->ex",
        collect,
        blocks.reshape(capacity, node_count, block_rows * hidden_width),
        precision=lax.Precision.HIGHEST,
    )
    gradient = lax.psum_scatter(
        summed.reshape(experts, block_rows, hidden_width).astype(jnp.bfloat16),
        "local",
        scatter_dimension=2,
        tiled=True,
    ).astype(jnp.float32)
    first_new = BETA_FIRST * first_moment + (1.0 - BETA_FIRST) * gradient
    second_new = BETA_SECOND * second_moment + (1.0 - BETA_SECOND) * gradient * gradient
    weight_old = master_weight.astype(jnp.float32)
    update = (
        first_new / CORRECT_FIRST / (jnp.sqrt(second_new / CORRECT_SECOND) + EPSILON)
        + DECAY_RATE * weight_old
    )
    weight_new = (weight_old - LEARNING_RATE * update).astype(jnp.bfloat16)
    choose = jnp.dot(
        one_hot(new_place, positions).T,
        one_hot(new_expert, experts),
        precision=lax.Precision.HIGHEST,
    )
    choose = choose.reshape(node_count, capacity, experts)
    flat_size = block_rows * columns
    send_weight = jnp.einsum(
        "nce,ex->cnx",
        choose.astype(jnp.bfloat16),
        weight_new.reshape(experts, flat_size),
        preferred_element_type=jnp.float32,
    ).astype(jnp.bfloat16)
    send_first = jnp.einsum(
        "nce,ex->cnx",
        choose,
        first_new.reshape(experts, flat_size),
        precision=lax.Precision.HIGHEST,
    )
    send_second = jnp.einsum(
        "nce,ex->cnx",
        choose,
        second_new.reshape(experts, flat_size),
        precision=lax.Precision.HIGHEST,
    )
    got_weight = lax.all_to_all(
        send_weight.reshape(capacity, node_count, block_rows, columns),
        "node",
        split_axis=1,
        concat_axis=1,
        tiled=True,
    )
    got_first, got_second = (
        lax.all_to_all(
            send_first.reshape(capacity, node_count, block_rows, columns),
            "node",
            split_axis=1,
            concat_axis=1,
            tiled=True,
        ),
        lax.all_to_all(
            send_second.reshape(capacity, node_count, block_rows, columns),
            "node",
            split_axis=1,
            concat_axis=1,
            tiled=True,
        ),
    )
    all_rows = node_count * block_rows
    return (
        got_weight.reshape(capacity, all_rows, columns),
        got_first.reshape(capacity, all_rows, columns),
        got_second.reshape(capacity, all_rows, columns),
    )


def solution(mesh):
    return jax.shard_map(
        local,
        mesh=mesh,
        in_specs=(
            P(None, "node", "local"),
            P(None, "node", "local"),
            P(None, "node", "local"),
            P("node", "local", None, None),
            P("node", "local", None, None),
            P(),
            P(),
            P(),
            P(),
        ),
        out_specs=(P("node", None, "local"), P("node", None, "local"), P("node", None, "local")),
        check_vma=False,
    )
```

profile of v0, /device:TPU:11, one launch (start us, length us, event | category | flops | bytes accessed | tf_op | source)
XLA Modules:
  0.0 350.1 jit_solution(8339204331855179574)
XLA Ops:
  9.1 1.9 fusion.3
  11.0 2.1 copy.59
  13.1 6.7 %all-to-all-start = ((bf16[6,16,8,2048]{3,2,0,1:T(8,128)(2,1)}), bf16[6,16,8,2048]{3,2,0,1:T(8,128)(2,1)S(1)}, u32[]{:S(2)}, u32[]{:S(2)}) async-start(bf16[6,16,8,2048]{3,2,0,1:T(8,128)(2,1)} %copy.59), calls=%async_computation | async-start | bytes 6291456 | tf_op jit(solution)/shard_map/all_to_all | solution.py:47
  20.2 69.4 %all-to-all-done = bf16[6,16,8,2048]{3,2,0,1:T(8,128)(2,1)S(1)} async-done(((bf16[6,16,8,2048]{3,2,0,1:T(8,128)(2,1)}), bf16[6,16,8,2048]{3,2,0,1:T(8,128)(2,1)S(1)}, u32[]{:S(2)}, u32[]{:S(2)}) %all-to-all-start) | async-done | bytes 3145760 | tf_op jit(solution)/shard_map/all_to_all | solution.py:47
  89.7 2.1 copy.60
  91.8 4.2 %reshape.60 = bf16[6,16,16384]{2,1,0:T(8,128)(2,1)S(1)} reshape(bf16[6,16,8,2048]{3,2,1,0:T(8,128)(2,1)} %copy.60) | data formatting | bytes 6291456 | tf_op jit(solution)/shard_map/reshape | solution.py:57
  96.0 3.1 bitcast_convert_fusion
  100.1 30.5 %reduce-scatter.2.cloned.1.call-done = bf16[64,8,1024]{2,0,1:T(8,128)(2,1)} async-done(((bf16[64,8,2048]{2,0,1:T(8,128)(2,1)}), bf16[64,8,1024]{2,0,1:T(8,128)(2,1)}) %reduce-scatter.2.cloned.1.call-update) | async-done | bytes 1048592 | tf_op jit(solution)/shard_map/reduce_scatter | solution.py:60
  130.6 8.7 %fusion.8 = (bf16[64,8,1024]{2,0,1:T(8,128)(2,1)S(1)}, f32[64,8,1024]{2,0,1:T(8,128)}, f32[64,8,1024]{2,0,1:T(8,128)}) fusion(bf16[64,8,1024]{2,1,0:T(8,128)(2,1)S(1)} %copy-done.4, bf16[64,8,1024]{2,0,1:T(8,128)(2,1)} %reduce-scatter.2.cloned.1.call-done, f32[64,8,1024]{2,1,0:T(8,128)} %param.10, f32[64,8,1024]{2,1,0:T(8,128)} %param.11), kind=kLoop, calls=%fused_computation.15 | loop fusion | flops 9437184 | bytes 11534336 | tf_op jit(solution)/shard_map/convert_element_type | solution.py:73
  145.3 6.4 %all-to-all-start.1 = ((bf16[6,16,8,1024]{3,2,0,1:T(8,128)(2,1)}), bf16[6,16,8,1024]{3,2,0,1:T(8,128)(2,1)}, u32[]{:S(2)}, u32[]{:S(2)}) async-start(bf16[6,16,8,1024]{3,2,0,1:T(8,128)(2,1)} %copy.67), calls=%async_computation.2 | async-start | bytes 3145728 | tf_op jit(solution)/shard_map/all_to_all | solution.py:99
  151.7 2.8 copy.74
  156.1 4.2 %fusion.16 = f32[8192,16,6]{0,1,2:T(8,128)S(1)} fusion(f32[64,8192,1]{1,0,2:T(8,128)} %reshape.75, f32[16,6,64]{2,1,0:T(8,128)S(1)} %reshape.65), kind=kOutput, calls=%fused_computation.30 | convolution fusion | flops 603979776 | bytes 5267456 | tf_op jit(solution)/shard_map/nce,ex->cnx/dot_general | solution.py:93
  160.3 2.2 copy.84
  164.4 23.5 %all-to-all-done.1 = bf16[6,16,8,1024]{3,2,0,1:T(8,128)(2,1)} async-done(((bf16[6,16,8,1024]{3,2,0,1:T(8,128)(2,1)}), bf16[6,16,8,1024]{3,2,0,1:T(8,128)(2,1)}, u32[]{:S(2)}, u32[]{:S(2)}) %all-to-all-start.1) | async-done | bytes 1572896 | tf_op jit(solution)/shard_map/all_to_all | solution.py:99
  187.9 4.9 %all-to-all-start.3 = ((f32[6,16,8,1024]{3,2,0,1:T(8,128)}), f32[6,16,8,1024]{3,2,0,1:T(8,128)S(1)}, u32[]{:S(2)}, u32[]{:S(2)}) async-start(f32[6,16,8,1024]{3,2,0,1:T(8,128)} %copy.76), calls=%async_computation.4 | async-start | bytes 6291456 | tf_op jit(solution)/shard_map/all_to_all | solution.py:114
  192.8 4.1 %copy.69 = f32[64,8,1024]{2,1,0:T(8,128)} copy(f32[64,8,1024]{2,0,1:T(8,128)} %get-tuple-element.4) | data formatting | bytes 4194304 | tf_op jit(solution)/shard_map/add | solution.py:66
  197.0 2.7 reshape.74
  199.7 4.3 %fusion.18 = f32[8192,16,6]{0,1,2:T(8,128)S(1)} fusion(f32[64,8192,1]{1,0,2:T(8,128)} %reshape.74, f32[16,6,64]{2,1,0:T(8,128)S(1)} %reshape.65), kind=kOutput, calls=%fused_computation.32 | convolution fusion | flops 603979776 | bytes 5267456 | tf_op jit(solution)/shard_map/nce,ex->cnx/dot_general | solution.py:87
  204.0 2.4 copy.83
  208.2 54.5 %all-to-all-done.3 = f32[6,16,8,1024]{3,2,0,1:T(8,128)S(1)} async-done(((f32[6,16,8,1024]{3,2,0,1:T(8,128)}), f32[6,16,8,1024]{3,2,0,1:T(8,128)S(1)}, u32[]{:S(2)}, u32[]{:S(2)}) %all-to-all-start.3) | async-done | bytes 3145760 | tf_op jit(solution)/shard_map/all_to_all | solution.py:114
  264.4 4.9 %all-to-all-start.2 = ((f32[6,16,8,1024]{3,2,0,1:T(8,128)}), f32[6,16,8,1024]{3,2,0,1:T(8,128)}, u32[]{:S(2)}, u32[]{:S(2)}) async-start(f32[6,16,8,1024]{3,2,0,1:T(8,128)} %copy.72), calls=%async_computation.3 | async-start | bytes 6291456 | tf_op jit(solution)/shard_map/all_to_all | solution.py:107
  269.3 2.9 copy.113
  274.0 65.2 %all-to-all-done.2 = f32[6,16,8,1024]{3,2,0,1:T(8,128)} async-done(((f32[6,16,8,1024]{3,2,0,1:T(8,128)}), f32[6,16,8,1024]{3,2,0,1:T(8,128)}, u32[]{:S(2)}, u32[]{:S(2)}) %all-to-all-start.2) | async-done | bytes 3145760 | tf_op jit(solution)/shard_map/all_to_all | solution.py:107
  339.3 4.0 %copy.112 = f32[6,16,8,1024]{3,2,1,0:T(8,128)} copy(f32[6,16,8,1024]{3,2,0,1:T(8,128)} %all-to-all-done.2) | data formatting | bytes 6291456 | tf_op jit(solution)/shard_map/all_to_all | solution.py:107
  (38 shorter events, 18.2 us)
Async XLA Ops:
  7.2 1.9 copy-start
  13.1 6.7 %copy-start.5 = (s32[16]{0:T(128)S(1)}, s32[16]{0:T(128)}, u32[]{:S(2)}) copy-start(s32[16]{0:T(128)} %param.17) | copy-start | bytes 196
  13.1 6.8 %copy-start.6 = (s32[16]{0:T(128)S(1)}, s32[16]{0:T(128)}, u32[]{:S(2)}) copy-start(s32[16]{0:T(128)} %param.16) | copy-start | bytes 196
  13.1 6.8 %copy-start.7 = (s32[80]{0:T(128)S(1)}, s32[80]{0:T(128)}, u32[]{:S(2)}) copy-start(s32[80]{0:T(128)} %param.14) | copy-start | bytes 964
  13.1 76.6 %all-to-all-start = ((bf16[6,16,8,2048]{3,2,0,1:T(8,128)(2,1)}), bf16[6,16,8,2048]{3,2,0,1:T(8,128)(2,1)S(1)}, u32[]{:S(2)}, u32[]{:S(2)}) async-start(bf16[6,16,8,2048]{3,2,0,1:T(8,128)(2,1)} %copy.59), calls=%async_computation | async-start | bytes 6291456 | tf_op jit(solution)/shard_map/all_to_all | solution.py:47
  19.8 110.8 %reduce-scatter.2.cloned.1.call-start = ((), (), s32[]{:S(2)}) async-start(), calls=%async_computation.5 | async-start | bytes 3145728 | tf_op jit(solution)/shard_map/reduce_scatter | solution.py:60
  99.0 0.7 copy-start.8
  99.0 31.5 %copy-start.4 = (bf16[64,8,1024]{2,1,0:T(8,128)(2,1)S(1)}, bf16[64,8,1024]{2,1,0:T(8,128)(2,1)}, u32[]{:S(2)}) copy-start(bf16[64,8,1024]{2,1,0:T(8,128)(2,1)} %param.9) | copy-start | bytes 3145732
  145.3 42.6 %all-to-all-start.1 = ((bf16[6,16,8,1024]{3,2,0,1:T(8,128)(2,1)}), bf16[6,16,8,1024]{3,2,0,1:T(8,128)(2,1)}, u32[]{:S(2)}, u32[]{:S(2)}) async-start(bf16[6,16,8,1024]{3,2,0,1:T(8,128)(2,1)} %copy.67), calls=%async_computation.2 | async-start | bytes 3145728 | tf_op jit(solution)/shard_map/all_to_all | solution.py:99
  187.9 74.8 %all-to-all-start.3 = ((f32[6,16,8,1024]{3,2,0,1:T(8,128)}), f32[6,16,8,1024]{3,2,0,1:T(8,128)S(1)}, u32[]{:S(2)}, u32[]{:S(2)}) async-start(f32[6,16,8,1024]{3,2,0,1:T(8,128)} %copy.76), calls=%async_computation.4 | async-start | bytes 6291456 | tf_op jit(solution)/shard_map/all_to_all | solution.py:114
  262.7 1.7 copy-start.2
  264.4 74.9 %all-to-all-start.2 = ((f32[6,16,8,1024]{3,2,0,1:T(8,128)}), f32[6,16,8,1024]{3,2,0,1:T(8,128)}, u32[]{:S(2)}, u32[]{:S(2)}) async-start(f32[6,16,8,1024]{3,2,0,1:T(8,128)} %copy.72), calls=%async_computation.3 | async-start | bytes 6291456 | tf_op jit(solution)/shard_map/all_to_all | solution.py:107
  269.3 2.9 copy-start.3
  272.2 71.1 %copy-start.1 = (bf16[6,1,128,2048]{3,2,1,0:T(8,128)(2,1)S(1)}, bf16[6,1,128,2048]{3,2,1,0:T(8,128)(2,1)}, u32[]{:S(2)}) copy-start(bf16[6,1,128,2048]{3,2,1,0:T(8,128)(2,1)} %param.13) | copy-start | bytes 9437188
Sparse Core Ops, SparseCore 0:
  99.2 31.3 reduce-scatter.1
where the time goes:
time: 351 us; the launch traced here: 350 us
  waiting for transfers between devices  243 us (69%)
  local copies, waits for them, and re-layouts  45.2 us (13%)
  starting transfers between devices  22.9 us (7%)
  matrix products  15.8 us (5%)
  between operations  14.2 us (4%)
  other arithmetic  8.8 us (3%)
    all_to_all x1, waiting for transfers between devices, local(): lax.all_to_all(slot_grad.reshape(capacity, node_count, block_rows, hidden...  69.4 us
    all_to_all x1, waiting for transfers between devices, local(): lax.all_to_all(send_first.reshape(capacity, node_count, block_rows, colum...  65.2 us
    all_to_all x1, waiting for transfers between devices, local(): lax.all_to_all(send_second.reshape(capacity, node_count, block_rows, colu...  54.5 us
    reduce_scatter x1, waiting for transfers between devices, local(): lax.psum_scatter(summed.reshape(experts, block_rows, hidden_width).astype...  30.5 us
    all_to_all x1, waiting for transfers between devices, local(): lax.all_to_all(send_weight.reshape(capacity, node_count, block_rows, colu...  23.5 us
    unnamed x21, local copies, waits for them, and re-layouts  9.73 us
    convert_element_type x1, other arithmetic, local(): weight_new = (weight_old - LEARNING_RATE * update).astype(jnp.bfloat16)  8.73 us
  transfers between devices with their start and end apart: 5, of which 5 were waited for; matrix products, arithmetic and copies ran while one was open for 10% of the time, Pallas kernels for 0%

commit v1 on v0

v1 whole, which is shorter than its diff:
```python
import functools

import jax
import jax.numpy as jnp
from jax import lax
from jax.experimental import pallas as pl
from jax.experimental.pallas import tpu as pltpu
from jax.sharding import PartitionSpec as P

BETA_FIRST = 0.9
BETA_SECOND = 0.95
LEARNING_RATE = 0.1
DECAY_RATE = 0.1
EPSILON = 1e-08
CORRECT_FIRST = 1.0 - 0.9**10
CORRECT_SECOND = 1.0 - 0.95**10

VMEM_LIMIT = 64 * 1024 * 1024
SMALL_LIMIT = 28 * 1024 * 1024


def position_table(place, expert, positions, empty):
    match = place[:, None] == jnp.arange(positions, dtype=jnp.int32)[None, :]
    held = jnp.sum(jnp.where(match, expert[:, None] + 1, 0), axis=0)
    return jnp.where(held > 0, held - 1, empty).astype(jnp.int32)


def moments(first_moment, second_moment, gradient):
    first_new = BETA_FIRST * first_moment + (1.0 - BETA_FIRST) * gradient
    second_new = BETA_SECOND * second_moment + (1.0 - BETA_SECOND) * gradient * gradient
    return first_new, second_new


def step_weight(weight_old, first_new, second_new):
    scaled = second_new * (1.0 / CORRECT_SECOND)
    root = scaled * lax.rsqrt(jnp.maximum(scaled, 1e-37))
    update = first_new * (1.0 / CORRECT_FIRST) / (root + EPSILON) + DECAY_RATE * weight_old
    return weight_old - LEARNING_RATE * update


def pair_gradient(nodes, features_ref, grad_ref):
    rows = features_ref.shape[3] // nodes
    parts = []
    for side in range(2):
        product = lax.dot_general(
            features_ref[side, 0],
            grad_ref[side, 0],
            (((0,), (0,)), ((), ())),
            preferred_element_type=jnp.float32,
        )
        parts.append(product.reshape(nodes, rows, product.shape[1]))
    return jnp.concatenate(parts, axis=1)


def front_kernel(side_ref, place_ref, owner_ref, features_ref, grad_ref, weight_ref, ahead_ref, theirs_ref, table):
    nodes = ahead_ref.shape[0]
    experts = weight_ref.shape[0]
    pair = pl.program_id(0)
    pairs = pl.num_programs(0)

    @pl.when(pair == 0)
    def _():
        @pl.loop(0, table.shape[0], unroll=16)
        def _(position):
            table[position] = experts

        @pl.loop(0, experts, unroll=16)
        def _(expert):
            table[place_ref[expert]] = expert

        @pl.loop(0, owner_ref.shape[0], unroll=16)
        def _(slot):
            table[place_ref[experts + slot]] = owner_ref[slot]

    theirs_ref[:, 0] = pair_gradient(nodes, features_ref, grad_ref).astype(jnp.bfloat16)
    for node in range(nodes):
        both = []
        for side in range(2):
            expert = table[(node * pairs + pair) * 2 + side]
            held = weight_ref[jnp.minimum(expert, experts - 1)].astype(jnp.float32)
            both.append(jnp.where(expert < experts, held, 0.0))
        ahead_ref[node, 0] = jnp.concatenate(both, axis=0).astype(jnp.bfloat16)


def front_call(nodes, side, new_place, new_owner, features, grad_out, weight):
    capacity, _, tokens, rows = features.shape
    columns = weight.shape[2]
    pairs = capacity // 2
    shape = jax.ShapeDtypeStruct((nodes, pairs, 2 * rows // nodes, columns), jnp.bfloat16)
    block = pl.BlockSpec((nodes, 1) + shape.shape[2:], lambda i, *_: (0, i, 0, 0))
    return pl.pallas_call(
        front_kernel,
        out_shape=[shape, shape],
        grid_spec=pltpu.PrefetchScalarGridSpec(
            num_scalar_prefetch=3,
            grid=(pairs,),
            in_specs=[
                pl.BlockSpec((2, 1, tokens, rows), lambda i, *_: (i, 0, 0, 0)),
                pl.BlockSpec((2, 1, tokens, columns), lambda i, s, *_: (i, 0, 0, 1 - s[0])),
                pl.BlockSpec(weight.shape, lambda i, *_: (0, 0, 0)),
            ],
            out_specs=[block, block],
            scratch_shapes=[pltpu.SMEM((nodes * capacity,), jnp.int32)],
        ),
        compiler_params=pltpu.CompilerParams(vmem_limit_bytes=VMEM_LIMIT),
        cost_estimate=pl.CostEstimate(
            flops=2 * capacity * tokens * rows * columns,
            bytes_accessed=8 * capacity * rows * columns,
            transcendentals=0,
        ),
    )(side, new_place, new_owner, features, grad_out, weight)


def without(kernel, first, after):
    return lambda *refs: kernel(*refs[:first], *refs[first + len(after) :])


def gradient_kernel(side_ref, features_ref, grad_ref, out_ref):
    out_ref[:, 0] = pair_gradient(out_ref.shape[0], features_ref, grad_ref).astype(jnp.bfloat16)


def gradient_call(nodes, side, features, grad_out, after):
    capacity, _, tokens, rows = features.shape
    columns = grad_out.shape[3] // 2
    pairs = capacity // 2
    shape = (nodes, pairs, 2 * rows // nodes, columns)
    return pl.pallas_call(
        without(gradient_kernel, 3, after),
        out_shape=jax.ShapeDtypeStruct(shape, jnp.bfloat16),
        grid_spec=pltpu.PrefetchScalarGridSpec(
            num_scalar_prefetch=1,
            grid=(pairs,),
            in_specs=[
                pl.BlockSpec((2, 1, tokens, rows), lambda i, s: (i, 0, 0, 0)),
                pl.BlockSpec((2, 1, tokens, columns), lambda i, s: (i, 0, 0, s[0])),
            ]
            + [pl.BlockSpec(memory_space=pl.ANY)] * len(after),
            out_specs=pl.BlockSpec((nodes, 1) + shape[2:], lambda i, s: (0, i, 0, 0)),
        ),
        compiler_params=pltpu.CompilerParams(vmem_limit_bytes=SMALL_LIMIT),
        cost_estimate=pl.CostEstimate(
            flops=2 * capacity * tokens * rows * columns,
            bytes_accessed=4 * capacity * rows * columns,
            transcendentals=0,
        ),
    )(side, features, grad_out, *after)


def arrived_kernel(ahead_ref, out_ref):
    out_ref[...] = jnp.zeros_like(out_ref)


def arrived_call(ahead):
    return pl.pallas_call(
        arrived_kernel,
        out_shape=jax.ShapeDtypeStruct((8, 128), jnp.float32),
        in_specs=[pl.BlockSpec(memory_space=pl.ANY)],
        compiler_params=pltpu.CompilerParams(vmem_limit_bytes=SMALL_LIMIT),
        cost_estimate=pl.CostEstimate(flops=0, bytes_accessed=4096, transcendentals=0),
    )(ahead)


def add_kernel(ours_ref, theirs_ref, out_ref):
    out_ref[...] = (ours_ref[...].astype(jnp.float32) + theirs_ref[...].astype(jnp.float32)).astype(jnp.bfloat16)


def add_call(ours, theirs, after):
    nodes, pairs, pair_rows, columns = ours.shape
    block = pl.BlockSpec((nodes, 1, pair_rows, columns), lambda i: (0, i, 0, 0))
    return pl.pallas_call(
        without(add_kernel, 2, after),
        out_shape=jax.ShapeDtypeStruct(ours.shape, jnp.bfloat16),
        grid=(pairs,),
        in_specs=[block, block] + [pl.BlockSpec(memory_space=pl.ANY)] * len(after),
        out_specs=block,
        compiler_params=pltpu.CompilerParams(vmem_limit_bytes=SMALL_LIMIT),
        cost_estimate=pl.CostEstimate(
            flops=nodes * pairs * pair_rows * columns,
            bytes_accessed=6 * nodes * pairs * pair_rows * columns,
            transcendentals=0,
        ),
    )(ours, theirs, *after)


def update_kernel(place_ref, owner_ref, new_ref, blocks_ref, first_ref, second_ref, send_ref, total, firsts, seconds):
    nodes = send_ref.shape[0]
    experts, rows, width = first_ref.shape
    pair = pl.program_id(0)
    pairs = pl.num_programs(0)

    def block_of(slot):
        position = place_ref[slot]
        both = blocks_ref[position // 2].astype(jnp.float32)
        return jnp.where(position % 2 == 1, both[rows:], both[:rows])

    @pl.when(pair == 0)
    def _():
        @pl.loop(0, experts, unroll=4)
        def _(expert):
            total[expert] = block_of(expert)

        @pl.loop(0, owner_ref.shape[0])
        def _(slot):
            expert = owner_ref[slot]
            total[expert] = total[expert] + block_of(experts + slot)

        @pl.loop(0, experts, unroll=4)
        def _(expert):
            first, second = moments(first_ref[expert], second_ref[expert], total[expert])
            firsts[expert] = first
            seconds[expert] = second

        for array in (firsts, seconds):
            array[experts] = jnp.zeros((rows, width), jnp.float32)

    for node in range(nodes):
        place = (node * pairs + pair) * 2
        left, right = new_ref[place], new_ref[place + 1]
        for which, array in enumerate((firsts, seconds)):
            both = jnp.concatenate([array[left], array[right]], axis=0)
            send_ref[node, which, 0] = both.astype(jnp.bfloat16)


def update_call(blocks, old_place, old_owner, new_table, first, second):
    nodes, pairs, pair_rows, columns = blocks.shape
    experts, rows, _ = first.shape
    whole = pl.BlockSpec(first.shape, lambda i, *_: (0, 0, 0))
    return pl.pallas_call(
        update_kernel,
        out_shape=jax.ShapeDtypeStruct((nodes, 2, pairs, pair_rows, columns), jnp.bfloat16),
        grid_spec=pltpu.PrefetchScalarGridSpec(
            num_scalar_prefetch=3,
            grid=(pairs,),
            in_specs=[
                pl.BlockSpec((nodes * pairs, pair_rows, columns), lambda i, *_: (0, 0, 0)),
                whole,
                whole,
            ],
            out_specs=pl.BlockSpec((nodes, 2, 1, pair_rows, columns), lambda i, *_: (0, 0, i, 0, 0)),
            scratch_shapes=[
                pltpu.VMEM((experts, rows, columns), jnp.float32),
                pltpu.VMEM((experts + 1, rows, columns), jnp.float32),
                pltpu.VMEM((experts + 1, rows, columns), jnp.float32),
            ],
        ),
        compiler_params=pltpu.CompilerParams(vmem_limit_bytes=SMALL_LIMIT),
        cost_estimate=pl.CostEstimate(
            flops=10 * experts * rows * columns,
            bytes_accessed=experts * rows * columns * 8 + 6 * nodes * pairs * pair_rows * columns,
            transcendentals=0,
        ),
    )(old_place, old_owner, new_table, blocks.reshape(nodes * pairs, pair_rows, columns), first, second)


def place_kernel(ahead_ref, got_ref, *out_refs):
    nodes, _, pair_rows, columns = ahead_ref.shape
    rows = pair_rows // 2
    for start in range(0, columns, 128):
        part = slice(start, start + 128)
        first, second = (got_ref[:, which, 0, :, part].astype(jnp.float32) for which in range(2))
        weight = step_weight(ahead_ref[:, 0, :, part].astype(jnp.float32), first, second)
        for out_ref, both in zip(out_refs, (weight, first, second)):
            for side in range(2):
                block = both[:, side * rows : (side + 1) * rows].reshape(nodes * rows, 128)
                out_ref[side, :, part] = block.astype(out_ref.dtype)


def place_call(ahead, got):
    nodes, pairs, pair_rows, columns = ahead.shape
    all_rows = nodes * pair_rows // 2
    return pl.pallas_call(
        place_kernel,
        out_shape=[
            jax.ShapeDtypeStruct((2 * pairs, all_rows, columns), dtype)
            for dtype in (jnp.bfloat16, jnp.float32, jnp.float32)
        ],
        grid=(pairs,),
        in_specs=[
            pl.BlockSpec((nodes, 1, pair_rows, columns), lambda i: (0, i, 0, 0)),
            pl.BlockSpec((nodes, 2, 1, pair_rows, columns), lambda i: (0, 0, i, 0, 0)),
        ],
        out_specs=[pl.BlockSpec((2, all_rows, columns), lambda i: (i, 0, 0))] * 3,
        compiler_params=pltpu.CompilerParams(vmem_limit_bytes=SMALL_LIMIT),
        cost_estimate=pl.CostEstimate(
            flops=20 * nodes * pairs * pair_rows * columns,
            bytes_accessed=16 * nodes * pairs * pair_rows * columns,
            transcendentals=0,
        ),
    )(ahead, got)


def exchange(array):
    return lax.all_to_all(array, "node", split_axis=0, concat_axis=0, tiled=True)


def paired(
    master_weight, first_moment, second_moment, features, grad_out, old_place, new_place, old_owner, new_owner, new_table
):
    nodes = lax.axis_size("node")
    side = jnp.reshape(lax.axis_index("local").astype(jnp.int32), (1,))
    ahead, theirs = front_call(nodes, side, new_place, new_owner, features, grad_out, master_weight)
    ahead = exchange(ahead)
    ours = gradient_call(nodes, side, features, grad_out, (theirs, new_table))
    theirs = lax.ppermute(theirs, "local", [(0, 1), (1, 0)])
    blocks = exchange(add_call(ours, theirs, (arrived_call(ahead),)))
    send = update_call(blocks, old_place, old_owner, new_table, first_moment, second_moment)
    return tuple(place_call(ahead, exchange(send)))


def plain(
    master_weight, first_moment, second_moment, features, grad_out, old_table, new_table
):
    nodes = lax.axis_size("node")
    capacity = features.shape[0]
    experts, rows, columns = master_weight.shape
    slot_grad = jnp.einsum("cltr,cltf->crf", features, grad_out, preferred_element_type=jnp.float32)
    part = lax.psum_scatter(
        slot_grad.astype(jnp.bfloat16), "local", scatter_dimension=2, tiled=True
    )
    part = part.reshape(capacity, nodes, rows, columns).transpose(1, 0, 2, 3)
    blocks = exchange(part).reshape(nodes * capacity, rows, columns).astype(jnp.float32)
    gradient = jnp.zeros((experts + 1, rows, columns), jnp.float32).at[old_table].add(blocks)[:experts]
    got = []
    for array in (master_weight, *moments(first_moment, second_moment, gradient)):
        padded = jnp.concatenate([array.astype(jnp.bfloat16), jnp.zeros((1, rows, columns), jnp.bfloat16)])
        sent = exchange(padded[new_table].reshape(nodes, capacity, rows, columns))
        sent = sent.transpose(1, 0, 2, 3).reshape(capacity, nodes * rows, columns)
        got.append(sent.astype(jnp.float32))
    return step_weight(*got).astype(jnp.bfloat16), got[1], got[2]


def local(
    master_weight,
    first_moment,
    second_moment,
    features,
    grad_out,
    old_place,
    new_place,
    old_owner,
    new_owner,
):
    nodes = lax.axis_size("node")
    capacity = features.shape[0]
    experts, rows, columns = master_weight.shape
    positions = nodes * capacity
    primaries = jnp.arange(experts, dtype=jnp.int32)
    new_table = position_table(new_place, jnp.concatenate([primaries, new_owner]), positions, experts)
    state = (master_weight, first_moment, second_moment, features, grad_out)
    if (
        lax.axis_size("local") == 2
        and capacity % 2 == 0
        and rows % 8 == 0
        and experts % 4 == 0
        and columns % 128 == 0
    ):
        return paired(*state, old_place, new_place, old_owner, new_owner, new_table)
    old_table = position_table(old_place, jnp.concatenate([primaries, old_owner]), positions, experts)
    return plain(*state, old_table, new_table)


def solution(mesh):
    return jax.shard_map(
        local,
        mesh=mesh,
        in_specs=(
            P(None, "node", "local"),
            P(None, "node", "local"),
            P(None, "node", "local"),
            P("node", "local", None, None),
            P("node", "local", None, None),
            P(),
            P(),
            P(),
            P(),
        ),
        out_specs=(P("node", None, "local"), P("node", None, "local"), P("node", None, "local")),
        check_vma=False,
    )
```

time: 351 us -> 177 us (0.50)
  waiting for transfers between devices: 243 us -> 32 us
  blocking collectives: 0 us -> 117 us
  local copies, waits for them, and re-layouts: 45.2 us -> 1.92 us
  Pallas kernels: 0 us -> 16 us
  matrix products: 15.8 us -> 0 us
  starting transfers between devices: 22.9 us -> 7.93 us
  between operations: 14.2 us -> 0.73 us
  other arithmetic: 8.8 us -> 0.18 us
    all_to_all x4 -> x1, waiting for transfers between devices: 213 us -> 32 us  [exchange(): lax.all_to_all(array, 'node', split_axis=0, concat_axis=0, tiled=True)]
    all_to_all x0 -> x2, blocking collectives: none -> 117 us  [exchange(): lax.all_to_all(array, 'node', split_axis=0, concat_axis=0, tiled=True)]
    reduce_scatter x1 -> x0, waiting for transfers between devices: 30.5 us -> none  [local(): lax.psum_scatter(summed.reshape(experts, block_rows, hidden_width).astype...]
    all_to_all x4 -> x1, starting transfers between devices: 22.9 us -> 6.7 us  [exchange(): lax.all_to_all(array, 'node', split_axis=0, concat_axis=0, tiled=True)]
    pallas_call x0 -> x6, Pallas kernels: none -> 16 us  [the longest x1 5.36 us: front_call(): pl.pallas_call(front_kernel, out_shape=[shape, shape], grid_spec=pltpu.Pr...]
    dot_general x7 -> x0, matrix products: 15.8 us -> none  [the longest x1 4.28 us: local(): jnp.einsum('nce,ex->cnx', choose, first_new.reshape(experts, flat_size),...]
    reshape x9 -> x0, local copies, waits for them, and re-layouts: 14.9 us -> none  [the longest x1 4.2 us: local(): blocks.reshape(capacity, node_count, block_rows * hidden_width)]
    all_to_all x4 -> x0, local copies, waits for them, and re-layouts: 10.8 us -> none  [the longest x1 3.97 us: local(): lax.all_to_all(send_first.reshape(capacity, node_count, block_rows, colum...]
  transfers between devices with their start and end apart: 5 -> 2, of which waited for: 5 -> 1; matrix products, arithmetic and copies ran while one was open for 10% -> 0% of each run, Pallas kernels for 0% -> 1%
where the time goes in v1:
time: 177 us; the launch traced here: 176 us
  blocking collectives  117 us (66%)
  waiting for transfers between devices  32 us (18%)
  Pallas kernels  16 us (9%)
  starting transfers between devices  7.93 us (4%)
  local copies, waits for them, and re-layouts  1.92 us (1%)
    all_to_all x2, blocking collectives, exchange(): lax.all_to_all(array, 'node', split_axis=0, concat_axis=0, tiled=True)  117 us
    all_to_all x1, waiting for transfers between devices, exchange(): lax.all_to_all(array, 'node', split_axis=0, concat_axis=0, tiled=True)  32 us
    all_to_all x1, starting transfers between devices, exchange(): lax.all_to_all(array, 'node', split_axis=0, concat_axis=0, tiled=True)  6.7 us
    pallas_call x1, Pallas kernels, front_call(): pl.pallas_call(front_kernel, out_shape=[shape, shape], grid_spec=pltpu.Pr...  5.36 us
    pallas_call x1, Pallas kernels, place_call(): pl.pallas_call(place_kernel, out_shape=[jax.ShapeDtypeStruct((2 * pairs,...  4.09 us
  transfers between devices with their start and end apart: 2, of which 1 were waited for; matrix products, arithmetic and copies ran while one was open for 0% of the time, Pallas kernels for 1%

profile of v1, /device:TPU:11, one launch (start us, length us, event | category | flops | bytes accessed | tf_op | source)
XLA Modules:
  0.0 175.6 jit_solution(13041976360874747037)
XLA Ops:
  0.6 5.4 %shard_map.112 = (bf16[16,3,16,1024]{3,2,1,0:T(8,128)(2,1)}, bf16[16,3,16,1024]{3,2,1,0:T(8,128)(2,1)}) custom-call(s32[1]{0:T(128)} %bitcast.side_ref.refs_0_, s32[80]{0:T(128)} %place_ref.2, s32[16]{0:T(128)} %owner_ref.2, bf16[6,1,128,128]{3,2,1,0:T(8,128)(2,1)} %refs_1_.1, bf16[6,1,128,2048]{3,2,1,0:T(8,128)(2,1)} %refs_2_.1, bf16[64,8,1024]{2,1,0:T(8,128)(2,1)} %weight_ref.1), custom_call_target="tpu_custom_call" | custom-call | flops 201326592 | bytes 6291456 | tf_op jit(solution)/shard_map/pallas_call | solution.py:91
  6.0 0.0 copy-start.3
  6.0 6.7 %all-to-all-start = ((bf16[16,3,16,1024]{3,2,1,0:T(8,128)(2,1)}), bf16[16,3,16,1024]{3,2,1,0:T(8,128)(2,1)S(1)}, u32[]{:S(2)}, u32[]{:S(2)}) async-start(bf16[16,3,16,1024]{3,2,1,0:T(8,128)(2,1)} %get-tuple-element.5), calls=%async_computation | async-start | bytes 3145728 | tf_op jit(solution)/shard_map/all_to_all | solution.py:293
  12.7 1.2 collective-permute-start
  14.0 0.0 copy-done.6
  14.0 0.1 add_add_fusion
  14.0 0.0 copy-done.7
  14.0 0.1 select_reduce_fusion
  14.1 0.0 copy-done.3
  14.2 0.0 copy-start
  14.2 1.9 %copy-done = bf16[6,1,128,2048]{3,2,1,0:T(8,128)(2,1)S(1)} copy-done((bf16[6,1,128,2048]{3,2,1,0:T(8,128)(2,1)S(1)}, bf16[6,1,128,2048]{3,2,1,0:T(8,128)(2,1)}, u32[]{:S(2)}) %copy-start) | copy-done | bytes 3145752
  16.0 1.2 shard_map.113.refs_0_
  17.3 32.0 %all-to-all-done.ahead_ref = bf16[16,3,16,1024]{3,2,1,0:T(8,128)(2,1)S(1)} async-done(((bf16[16,3,16,1024]{3,2,1,0:T(8,128)(2,1)}), bf16[16,3,16,1024]{3,2,1,0:T(8,128)(2,1)S(1)}, u32[]{:S(2)}, u32[]{:S(2)}) %all-to-all-start) | async-done | bytes 1572896 | tf_op jit(solution)/shard_map/all_to_all | solution.py:293
  49.3 0.0 collective-permute-done.refs_1_
  49.3 2.6 %shard_map.115 = bf16[16,3,16,1024]{3,2,1,0:T(8,128)(2,1)S(1)} custom-call(bf16[16,3,16,1024]{3,2,1,0:T(8,128)(2,1)S(1)} %shard_map.113.refs_0_, bf16[16,3,16,1024]{3,2,1,0:T(8,128)(2,1)} %collective-permute-done.refs_1_, f32[8,128]{1,0:T(8,128)S(1)} %shard_map.114.refs_2_), custom_call_target="tpu_custom_call" | custom-call | flops 786432 | bytes 4718592 | tf_op jit(solution)/shard_map/pallas_call | solution.py:170
  52.0 0.0 copy-start.1
  52.0 0.0 copy-start.4
  52.0 0.0 copy-start.5
  52.0 42.2 %all_to_all.15 = bf16[16,3,16,1024]{3,2,1,0:T(8,128)(2,1)S(1)} all-to-all(bf16[16,3,16,1024]{3,2,1,0:T(8,128)(2,1)S(1)} %shard_map.115), channel_id=1, replica_groups=mesh['node'=16,'local'=2] {'node'}, dimensions={0} | all-to-all | bytes 3145728 | tf_op jit(solution)/shard_map/all_to_all | solution.py:293
  94.2 0.0 copy-done.2
  94.2 0.0 copy-done.1
  94.2 2.6 %shard_map.116 = bf16[16,2,3,16,1024]{4,3,2,1,0:T(8,128)(2,1)S(1)} custom-call(s32[80]{0:T(128)S(1)} %copy-done.4, s32[16]{0:T(128)S(1)} %copy-done.5, s32[96]{0:T(128)S(1)} %compare_select_fusion.refs_4_.new_ref, bf16[48,16,1024]{2,1,0:T(8,128)(2,1)S(1)} %bitcast.2, f32[64,8,1024]{2,1,0:T(8,128)S(1)} %copy-done.1, f32[64,8,1024]{2,1,0:T(8,128)S(1)} %copy-done.2), custom_call_target="tpu_custom_call" | custom-call | flops 5242880 | bytes 8912896 | tf_op jit(solution)/shard_map/pallas_call | solution.py:228
  96.9 74.6 %all_to_all.16.got_ref = bf16[16,2,3,16,1024]{4,3,2,1,0:T(8,128)(2,1)S(1)} all-to-all(bf16[16,2,3,16,1024]{4,3,2,1,0:T(8,128)(2,1)S(1)} %shard_map.116), channel_id=1, replica_groups=mesh['node'=16,'local'=2] {'node'}, dimensions={0} | all-to-all | bytes 6291456 | tf_op jit(solution)/shard_map/all_to_all | solution.py:293
  171.5 4.1 %shard_map.117 = (bf16[6,128,1024]{2,1,0:T(8,128)(2,1)}, f32[6,128,1024]{2,1,0:T(8,128)}, f32[6,128,1024]{2,1,0:T(8,128)}) custom-call(bf16[16,3,16,1024]{3,2,1,0:T(8,128)(2,1)S(1)} %all-to-all-done.ahead_ref, bf16[16,2,3,16,1024]{4,3,2,1,0:T(8,128)(2,1)S(1)} %all_to_all.16.got_ref), custom_call_target="tpu_custom_call" | custom-call | flops 15728640 | bytes 12582912 | tf_op jit(solution)/shard_map/pallas_call | solution.py:271
  (8 shorter events, 0.0 us)
Async XLA Ops:
  6.0 8.0 %copy-start.6 = (s32[16]{0:T(128)S(1)}, s32[16]{0:T(128)}, u32[]{:S(2)}) copy-start(s32[16]{0:T(128)} %owner_ref.2) | copy-start | bytes 196
  6.0 8.0 %copy-start.7 = (s32[80]{0:T(128)S(1)}, s32[80]{0:T(128)}, u32[]{:S(2)}) copy-start(s32[80]{0:T(128)} %place_ref.2) | copy-start | bytes 964
  6.0 8.1 %copy-start.3 = (bf16[6,1,128,128]{3,2,1,0:T(8,128)(2,1)S(1)}, bf16[6,1,128,128]{3,2,1,0:T(8,128)(2,1)}, u32[]{:S(2)}) copy-start(bf16[6,1,128,128]{3,2,1,0:T(8,128)(2,1)} %refs_1_.1) | copy-start | bytes 589828
  6.0 43.3 %all-to-all-start = ((bf16[16,3,16,1024]{3,2,1,0:T(8,128)(2,1)}), bf16[16,3,16,1024]{3,2,1,0:T(8,128)(2,1)S(1)}, u32[]{:S(2)}, u32[]{:S(2)}) async-start(bf16[16,3,16,1024]{3,2,1,0:T(8,128)(2,1)} %get-tuple-element.5), calls=%async_computation | async-start | bytes 3145728 | tf_op jit(solution)/shard_map/all_to_all | solution.py:293
  12.7 36.6 %collective-permute-start = (bf16[16,3,16,1024]{3,2,1,0:T(8,128)(2,1)}, bf16[16,3,16,1024]{3,2,1,0:T(8,128)(2,1)}, u32[]{:S(2)}, u32[]{:S(2)}) collective-permute-start(bf16[16,3,16,1024]{3,2,1,0:T(8,128)(2,1)} %get-tuple-element.6.refs_3_), channel_id=1, source_target_pairs={{0,1},{1,0},{2,3},{3,2},{4,5},{5,4},{6,7},{7,6},{8,9},{9,8},{10,11... | collective-permute-start | bytes 4718600 | tf_op jit(solution)/shard_map/ppermute | solution.py:304
  14.2 1.9 %copy-start = (bf16[6,1,128,2048]{3,2,1,0:T(8,128)(2,1)S(1)}, bf16[6,1,128,2048]{3,2,1,0:T(8,128)(2,1)}, u32[]{:S(2)}) copy-start(bf16[6,1,128,2048]{3,2,1,0:T(8,128)(2,1)} %refs_2_.1) | copy-start | bytes 9437188
  49.3 44.9 %copy-start.2 = (f32[64,8,1024]{2,1,0:T(8,128)S(1)}, f32[64,8,1024]{2,1,0:T(8,128)}, u32[]{:S(2)}) copy-start(f32[64,8,1024]{2,1,0:T(8,128)} %second_ref.1) | copy-start | bytes 6291460
  52.0 42.2 %copy-start.1 = (f32[64,8,1024]{2,1,0:T(8,128)S(1)}, f32[64,8,1024]{2,1,0:T(8,128)}, u32[]{:S(2)}) copy-start(f32[64,8,1024]{2,1,0:T(8,128)} %first_ref.1) | copy-start | bytes 6291460
  52.0 42.2 %copy-start.4 = (s32[80]{0:T(128)S(1)}, s32[80]{0:T(128)}, u32[]{:S(2)}) copy-start(s32[80]{0:T(128)} %place_ref.3) | copy-start | bytes 964
  52.0 42.2 %copy-start.5 = (s32[16]{0:T(128)S(1)}, s32[16]{0:T(128)}, u32[]{:S(2)}) copy-start(s32[16]{0:T(128)} %owner_ref.3) | copy-start | bytes 196

commit v2 on v1

--- a/solution.py
+++ b/solution.py
@@ -60,16 +60,11 @@
 
     @pl.when(pair == 0)
     def _():
-        @pl.loop(0, table.shape[0], unroll=16)
-        def _(position):
+        for position in range(table.shape[0]):
             table[position] = experts
-
-        @pl.loop(0, experts, unroll=16)
-        def _(expert):
+        for expert in range(experts):
             table[place_ref[expert]] = expert
-
-        @pl.loop(0, owner_ref.shape[0], unroll=16)
-        def _(slot):
+        for slot in range(owner_ref.shape[0]):
             table[place_ref[experts + slot]] = owner_ref[slot]
 
     theirs_ref[:, 0] = pair_gradient(nodes, features_ref, grad_ref).astype(jnp.bfloat16)

time: 177 us -> 177 us (level)
  no operation moved by 1% of the time
where the time goes in v2:
time: 177 us; the launch traced here: 176 us
  blocking collectives  117 us (66%)
  waiting for transfers between devices  32 us (18%)
  Pallas kernels  16 us (9%)
  starting transfers between devices  7.93 us (4%)
  local copies, waits for them, and re-layouts  1.92 us (1%)
    all_to_all x2, blocking collectives, exchange(): lax.all_to_all(array, 'node', split_axis=0, concat_axis=0, tiled=True)  117 us
    all_to_all x1, waiting for transfers between devices, exchange(): lax.all_to_all(array, 'node', split_axis=0, concat_axis=0, tiled=True)  32 us
    all_to_all x1, starting transfers between devices, exchange(): lax.all_to_all(array, 'node', split_axis=0, concat_axis=0, tiled=True)  6.7 us
    pallas_call x1, Pallas kernels, front_call(): pl.pallas_call(front_kernel, out_shape=[shape, shape], grid_spec=pltpu.Pr...  5.36 us
    pallas_call x1, Pallas kernels, place_call(): pl.pallas_call(place_kernel, out_shape=[jax.ShapeDtypeStruct((2 * pairs,...  4.09 us
  transfers between devices with their start and end apart: 2, of which 1 were waited for; matrix products, arithmetic and copies ran while one was open for 0% of the time, Pallas kernels for 1%

profile of v2, /device:TPU:11, one launch (start us, length us, event | category | flops | bytes accessed | tf_op | source)
XLA Modules:
  0.0 175.6 jit_solution(3639323877992746351)
XLA Ops:
  0.6 5.4 %shard_map.112 = (bf16[16,3,16,1024]{3,2,1,0:T(8,128)(2,1)}, bf16[16,3,16,1024]{3,2,1,0:T(8,128)(2,1)}) custom-call(s32[1]{0:T(128)} %bitcast.side_ref.refs_0_, s32[80]{0:T(128)} %place_ref.2, s32[16]{0:T(128)} %owner_ref.2, bf16[6,1,128,128]{3,2,1,0:T(8,128)(2,1)} %refs_1_.1, bf16[6,1,128,2048]{3,2,1,0:T(8,128)(2,1)} %refs_2_.1, bf16[64,8,1024]{2,1,0:T(8,128)(2,1)} %weight_ref.1), custom_call_target="tpu_custom_call" | custom-call | flops 201326592 | bytes 6291456 | tf_op jit(solution)/shard_map/pallas_call | solution.py:86
  6.0 0.0 copy-start.3
  6.0 6.7 %all-to-all-start = ((bf16[16,3,16,1024]{3,2,1,0:T(8,128)(2,1)}), bf16[16,3,16,1024]{3,2,1,0:T(8,128)(2,1)S(1)}, u32[]{:S(2)}, u32[]{:S(2)}) async-start(bf16[16,3,16,1024]{3,2,1,0:T(8,128)(2,1)} %get-tuple-element.5), calls=%async_computation | async-start | bytes 3145728 | tf_op jit(solution)/shard_map/all_to_all | solution.py:288
  12.7 1.2 collective-permute-start
  14.0 0.0 copy-done.6
  14.0 0.1 add_add_fusion
  14.0 0.0 copy-done.7
  14.0 0.1 select_reduce_fusion
  14.1 0.0 copy-done.3
  14.2 0.0 copy-start
  14.2 1.9 %copy-done = bf16[6,1,128,2048]{3,2,1,0:T(8,128)(2,1)S(1)} copy-done((bf16[6,1,128,2048]{3,2,1,0:T(8,128)(2,1)S(1)}, bf16[6,1,128,2048]{3,2,1,0:T(8,128)(2,1)}, u32[]{:S(2)}) %copy-start) | copy-done | bytes 3145752
  16.0 1.2 shard_map.113.refs_0_
  17.3 32.0 %all-to-all-done.ahead_ref = bf16[16,3,16,1024]{3,2,1,0:T(8,128)(2,1)S(1)} async-done(((bf16[16,3,16,1024]{3,2,1,0:T(8,128)(2,1)}), bf16[16,3,16,1024]{3,2,1,0:T(8,128)(2,1)S(1)}, u32[]{:S(2)}, u32[]{:S(2)}) %all-to-all-start) | async-done | bytes 1572896 | tf_op jit(solution)/shard_map/all_to_all | solution.py:288
  49.3 0.0 collective-permute-done.refs_1_
  49.3 2.6 %shard_map.115 = bf16[16,3,16,1024]{3,2,1,0:T(8,128)(2,1)S(1)} custom-call(bf16[16,3,16,1024]{3,2,1,0:T(8,128)(2,1)S(1)} %shard_map.113.refs_0_, bf16[16,3,16,1024]{3,2,1,0:T(8,128)(2,1)} %collective-permute-done.refs_1_, f32[8,128]{1,0:T(8,128)S(1)} %shard_map.114.refs_2_), custom_call_target="tpu_custom_call" | custom-call | flops 786432 | bytes 4718592 | tf_op jit(solution)/shard_map/pallas_call | solution.py:165
  52.0 0.0 copy-start.1
  52.0 0.0 copy-start.4
  52.0 0.0 copy-start.5
  52.0 42.2 %all_to_all.15 = bf16[16,3,16,1024]{3,2,1,0:T(8,128)(2,1)S(1)} all-to-all(bf16[16,3,16,1024]{3,2,1,0:T(8,128)(2,1)S(1)} %shard_map.115), channel_id=1, replica_groups=mesh['node'=16,'local'=2] {'node'}, dimensions={0} | all-to-all | bytes 3145728 | tf_op jit(solution)/shard_map/all_to_all | solution.py:288
  94.2 0.0 copy-done.2
  94.2 0.0 copy-done.1
  94.2 2.6 %shard_map.116 = bf16[16,2,3,16,1024]{4,3,2,1,0:T(8,128)(2,1)S(1)} custom-call(s32[80]{0:T(128)S(1)} %copy-done.4, s32[16]{0:T(128)S(1)} %copy-done.5, s32[96]{0:T(128)S(1)} %compare_select_fusion.refs_4_.new_ref, bf16[48,16,1024]{2,1,0:T(8,128)(2,1)S(1)} %bitcast.2, f32[64,8,1024]{2,1,0:T(8,128)S(1)} %copy-done.1, f32[64,8,1024]{2,1,0:T(8,128)S(1)} %copy-done.2), custom_call_target="tpu_custom_call" | custom-call | flops 5242880 | bytes 8912896 | tf_op jit(solution)/shard_map/pallas_call | solution.py:223
  96.9 74.6 %all_to_all.16.got_ref = bf16[16,2,3,16,1024]{4,3,2,1,0:T(8,128)(2,1)S(1)} all-to-all(bf16[16,2,3,16,1024]{4,3,2,1,0:T(8,128)(2,1)S(1)} %shard_map.116), channel_id=1, replica_groups=mesh['node'=16,'local'=2] {'node'}, dimensions={0} | all-to-all | bytes 6291456 | tf_op jit(solution)/shard_map/all_to_all | solution.py:288
  171.5 4.1 %shard_map.117 = (bf16[6,128,1024]{2,1,0:T(8,128)(2,1)}, f32[6,128,1024]{2,1,0:T(8,128)}, f32[6,128,1024]{2,1,0:T(8,128)}) custom-call(bf16[16,3,16,1024]{3,2,1,0:T(8,128)(2,1)S(1)} %all-to-all-done.ahead_ref, bf16[16,2,3,16,1024]{4,3,2,1,0:T(8,128)(2,1)S(1)} %all_to_all.16.got_ref), custom_call_target="tpu_custom_call" | custom-call | flops 15728640 | bytes 12582912 | tf_op jit(solution)/shard_map/pallas_call | solution.py:266
  (8 shorter events, 0.0 us)
Async XLA Ops:
  6.0 8.0 %copy-start.6 = (s32[16]{0:T(128)S(1)}, s32[16]{0:T(128)}, u32[]{:S(2)}) copy-start(s32[16]{0:T(128)} %owner_ref.2) | copy-start | bytes 196
  6.0 8.0 %copy-start.7 = (s32[80]{0:T(128)S(1)}, s32[80]{0:T(128)}, u32[]{:S(2)}) copy-start(s32[80]{0:T(128)} %place_ref.2) | copy-start | bytes 964
  6.0 8.1 %copy-start.3 = (bf16[6,1,128,128]{3,2,1,0:T(8,128)(2,1)S(1)}, bf16[6,1,128,128]{3,2,1,0:T(8,128)(2,1)}, u32[]{:S(2)}) copy-start(bf16[6,1,128,128]{3,2,1,0:T(8,128)(2,1)} %refs_1_.1) | copy-start | bytes 589828
  6.0 43.3 %all-to-all-start = ((bf16[16,3,16,1024]{3,2,1,0:T(8,128)(2,1)}), bf16[16,3,16,1024]{3,2,1,0:T(8,128)(2,1)S(1)}, u32[]{:S(2)}, u32[]{:S(2)}) async-start(bf16[16,3,16,1024]{3,2,1,0:T(8,128)(2,1)} %get-tuple-element.5), calls=%async_computation | async-start | bytes 3145728 | tf_op jit(solution)/shard_map/all_to_all | solution.py:288
  12.7 36.6 %collective-permute-start = (bf16[16,3,16,1024]{3,2,1,0:T(8,128)(2,1)}, bf16[16,3,16,1024]{3,2,1,0:T(8,128)(2,1)}, u32[]{:S(2)}, u32[]{:S(2)}) collective-permute-start(bf16[16,3,16,1024]{3,2,1,0:T(8,128)(2,1)} %get-tuple-element.6.refs_3_), channel_id=1, source_target_pairs={{0,1},{1,0},{2,3},{3,2},{4,5},{5,4},{6,7},{7,6},{8,9},{9,8},{10,11... | collective-permute-start | bytes 4718600 | tf_op jit(solution)/shard_map/ppermute | solution.py:299
  14.2 1.9 %copy-start = (bf16[6,1,128,2048]{3,2,1,0:T(8,128)(2,1)S(1)}, bf16[6,1,128,2048]{3,2,1,0:T(8,128)(2,1)}, u32[]{:S(2)}) copy-start(bf16[6,1,128,2048]{3,2,1,0:T(8,128)(2,1)} %refs_2_.1) | copy-start | bytes 9437188
  49.3 44.9 %copy-start.2 = (f32[64,8,1024]{2,1,0:T(8,128)S(1)}, f32[64,8,1024]{2,1,0:T(8,128)}, u32[]{:S(2)}) copy-start(f32[64,8,1024]{2,1,0:T(8,128)} %second_ref.1) | copy-start | bytes 6291460
  52.0 42.2 %copy-start.1 = (f32[64,8,1024]{2,1,0:T(8,128)S(1)}, f32[64,8,1024]{2,1,0:T(8,128)}, u32[]{:S(2)}) copy-start(f32[64,8,1024]{2,1,0:T(8,128)} %first_ref.1) | copy-start | bytes 6291460
  52.0 42.2 %copy-start.4 = (s32[80]{0:T(128)S(1)}, s32[80]{0:T(128)}, u32[]{:S(2)}) copy-start(s32[80]{0:T(128)} %place_ref.3) | copy-start | bytes 964
  52.0 42.2 %copy-start.5 = (s32[16]{0:T(128)S(1)}, s32[16]{0:T(128)}, u32[]{:S(2)}) copy-start(s32[16]{0:T(128)} %owner_ref.3) | copy-start | bytes 196

commit v3 on v2

--- a/solution.py
+++ b/solution.py
@@ -52,7 +52,7 @@
     return jnp.concatenate(parts, axis=1)
 
 
-def front_kernel(side_ref, place_ref, owner_ref, features_ref, grad_ref, weight_ref, ahead_ref, theirs_ref, table):
+def front_kernel(side_ref, place_ref, owner_ref, features_ref, grad_ref, weight_ref, ahead_ref, low_ref, high_ref, table):
     nodes = ahead_ref.shape[0]
     experts = weight_ref.shape[0]
     pair = pl.program_id(0)
@@ -67,7 +67,10 @@
         for slot in range(owner_ref.shape[0]):
             table[place_ref[experts + slot]] = owner_ref[slot]
 
-    theirs_ref[:, 0] = pair_gradient(nodes, features_ref, grad_ref).astype(jnp.bfloat16)
+    theirs = pair_gradient(nodes, features_ref, grad_ref).astype(jnp.bfloat16)
+    width = low_ref.shape[3]
+    low_ref[:, 0] = theirs[:, :, :width]
+    high_ref[:, 0] = theirs[:, :, width:]
     for node in range(nodes):
         both = []
         for side in range(2):
@@ -83,9 +86,11 @@
     pairs = capacity // 2
     shape = jax.ShapeDtypeStruct((nodes, pairs, 2 * rows // nodes, columns), jnp.bfloat16)
     block = pl.BlockSpec((nodes, 1) + shape.shape[2:], lambda i, *_: (0, i, 0, 0))
+    part = jax.ShapeDtypeStruct(shape.shape[:3] + (columns // 2,), jnp.bfloat16)
+    part_block = pl.BlockSpec((nodes, 1) + part.shape[2:], lambda i, *_: (0, i, 0, 0))
     return pl.pallas_call(
         front_kernel,
-        out_shape=[shape, shape],
+        out_shape=[shape, part, part],
         grid_spec=pltpu.PrefetchScalarGridSpec(
             num_scalar_prefetch=3,
             grid=(pairs,),
@@ -94,7 +99,7 @@
                 pl.BlockSpec((2, 1, tokens, columns), lambda i, s, *_: (i, 0, 0, 1 - s[0])),
                 pl.BlockSpec(weight.shape, lambda i, *_: (0, 0, 0)),
             ],
-            out_specs=[block, block],
+            out_specs=[block, part_block, part_block],
             scratch_shapes=[pltpu.SMEM((nodes * capacity,), jnp.int32)],
         ),
         compiler_params=pltpu.CompilerParams(vmem_limit_bytes=VMEM_LIMIT),
@@ -159,22 +164,25 @@
     out_ref[...] = (ours_ref[...].astype(jnp.float32) + theirs_ref[...].astype(jnp.float32)).astype(jnp.bfloat16)
 
 
-def add_call(ours, theirs, after):
-    nodes, pairs, pair_rows, columns = ours.shape
-    block = pl.BlockSpec((nodes, 1, pair_rows, columns), lambda i: (0, i, 0, 0))
-    return pl.pallas_call(
-        without(add_kernel, 2, after),
+def add_call(which, ours, theirs, before=(), after=()):
+    nodes, pairs, pair_rows, width = theirs.shape
+    block = pl.BlockSpec((nodes, 1, pair_rows, width), lambda i: (0, i, 0, 0))
+    side = pl.BlockSpec((nodes, 1, pair_rows, width), lambda i: (0, i, 0, which))
+    unread = (*before, *after)
+    return pl.pallas_call(
+        without(add_kernel, 2, unread),
         out_shape=jax.ShapeDtypeStruct(ours.shape, jnp.bfloat16),
         grid=(pairs,),
-        in_specs=[block, block] + [pl.BlockSpec(memory_space=pl.ANY)] * len(after),
-        out_specs=block,
-        compiler_params=pltpu.CompilerParams(vmem_limit_bytes=SMALL_LIMIT),
-        cost_estimate=pl.CostEstimate(
-            flops=nodes * pairs * pair_rows * columns,
-            bytes_accessed=6 * nodes * pairs * pair_rows * columns,
-            transcendentals=0,
-        ),
-    )(ours, theirs, *after)
+        in_specs=[side, block] + [pl.BlockSpec(memory_space=pl.ANY)] * len(unread),
+        out_specs=side,
+        input_output_aliases={2: 0} if before else {},
+        compiler_params=pltpu.CompilerParams(vmem_limit_bytes=SMALL_LIMIT),
+        cost_estimate=pl.CostEstimate(
+            flops=nodes * pairs * pair_rows * width,
+            bytes_accessed=6 * nodes * pairs * pair_rows * width,
+            transcendentals=0,
+        ),
+    )(ours, theirs, *unread)
 
 
 def update_kernel(place_ref, owner_ref, new_ref, blocks_ref, first_ref, second_ref, send_ref, total, firsts, seconds):
@@ -293,11 +301,12 @@
 ):
     nodes = lax.axis_size("node")
     side = jnp.reshape(lax.axis_index("local").astype(jnp.int32), (1,))
-    ahead, theirs = front_call(nodes, side, new_place, new_owner, features, grad_out, master_weight)
+    ahead, *theirs = front_call(nodes, side, new_place, new_owner, features, grad_out, master_weight)
     ahead = exchange(ahead)
-    ours = gradient_call(nodes, side, features, grad_out, (theirs, new_table))
-    theirs = lax.ppermute(theirs, "local", [(0, 1), (1, 0)])
-    blocks = exchange(add_call(ours, theirs, (arrived_call(ahead),)))
+    ours = gradient_call(nodes, side, features, grad_out, (*theirs, new_table))
+    low, high = (lax.ppermute(part, "local", [(0, 1), (1, 0)]) for part in theirs)
+    blocks = add_call(0, ours, low)
+    blocks = exchange(add_call(1, ours, high, (blocks,), (arrived_call(ahead),)))
     send = update_call(blocks, old_place, old_owner, new_table, first_moment, second_moment)
     return tuple(place_call(ahead, exchange(send)))
 
@@ -347,7 +356,7 @@
         and capacity % 2 == 0
         and rows % 8 == 0
         and experts % 4 == 0
-        and columns % 128 == 0
+        and columns % 256 == 0
     ):
         return paired(*state, old_place, new_place, old_owner, new_owner, new_table)
     old_table = position_table(old_place, jnp.concatenate([primaries, old_owner]), positions, experts)

time: 177 us -> 177 us (level)
  local copies, waits for them, and re-layouts: 1.92 us -> 4.47 us
  blocking collectives: 117 us -> 115 us
  waiting for transfers between devices: 32 us -> 30.2 us
    all_to_all x1, waiting for transfers between devices: 32 us -> 16.2 us  [exchange(): lax.all_to_all(array, 'node', split_axis=0, concat_axis=0, tiled=True)]
    ppermute x1 -> x2, waiting for transfers between devices: 0.01 us -> 14 us  [paired(): lax.ppermute(part, 'local', [(0, 1), (1, 0)])]
    unnamed x16 -> x22, local copies, waits for them, and re-layouts: 1.92 us -> 4.47 us
    pallas_call x2 -> x3, Pallas kernels: 8 us -> 8.05 us  [the longest x1 5.38 us: front_call(): pl.pallas_call(front_kernel, out_shape=[shape, part, part], grid_spec=plt...]
  transfers between devices with their start and end apart: 2 -> 3, of which waited for: 1 -> 2; matrix products, arithmetic and copies ran while one was open for 0% -> 0% of each run, Pallas kernels for 1% -> 1%
where the time goes in v3:
time: 177 us; the launch traced here: 175 us
  blocking collectives  115 us (65%)
  waiting for transfers between devices  30.2 us (17%)
  Pallas kernels  16.1 us (9%)
  starting transfers between devices  8.23 us (5%)
  local copies, waits for them, and re-layouts  4.47 us (3%)
    all_to_all x2, blocking collectives, exchange(): lax.all_to_all(array, 'node', split_axis=0, concat_axis=0, tiled=True)  115 us
    all_to_all x1, waiting for transfers between devices, exchange(): lax.all_to_all(array, 'node', split_axis=0, concat_axis=0, tiled=True)  16.2 us
    ppermute x2, waiting for transfers between devices, paired(): lax.ppermute(part, 'local', [(0, 1), (1, 0)])  14 us
    all_to_all x1, starting transfers between devices, exchange(): lax.all_to_all(array, 'node', split_axis=0, concat_axis=0, tiled=True)  6.7 us
    pallas_call x1, Pallas kernels, front_call(): pl.pallas_call(front_kernel, out_shape=[shape, part, part], grid_spec=plt...  5.38 us
    unnamed x22, local copies, waits for them, and re-layouts  4.47 us
    pallas_call x1, Pallas kernels, place_call(): pl.pallas_call(place_kernel, out_shape=[jax.ShapeDtypeStruct((2 * pairs,...  4.09 us
  transfers between devices with their start and end apart: 3, of which 2 were waited for; matrix products, arithmetic and copies ran while one was open for 0% of the time, Pallas kernels for 1%

profile of v3, /device:TPU:11, one launch (start us, length us, event | category | flops | bytes accessed | tf_op | source)
XLA Modules:
  0.0 175.1 jit_solution(10097621723612214898)
XLA Ops:
  0.6 5.4 %shard_map.112 = (bf16[16,3,16,1024]{3,2,1,0:T(8,128)(2,1)}, bf16[16,3,16,512]{3,2,1,0:T(8,128)(2,1)}, bf16[16,3,16,512]{3,2,1,0:T(8,128)(2,1)}) custom-call(s32[1]{0:T(128)} %bitcast.side_ref.refs_0_, s32[80]{0:T(128)} %place_ref.2, s32[16]{0:T(128)} %owner_ref.2, bf16[6,1,128,128]{3,2,1,0:T(8,128)(2,1)} %refs_1_.1, bf16[6,1,128,2048]{3,2,1,0:T(8,128)(2,1)} %refs_2_.1, ...), custom_call_target="tpu_custom_call" | custom-call | flops 201326592 | bytes 6291456 | tf_op jit(solution)/shard_map/pallas_call | solution.py:91
  6.0 0.0 copy-start.10
  6.0 0.0 copy-start.5
  6.0 6.7 %all-to-all-start = ((bf16[16,3,16,1024]{3,2,1,0:T(8,128)(2,1)}), bf16[16,3,16,1024]{3,2,1,0:T(8,128)(2,1)S(1)}, u32[]{:S(2)}, u32[]{:S(2)}) async-start(bf16[16,3,16,1024]{3,2,1,0:T(8,128)(2,1)} %get-tuple-element.6), calls=%async_computation | async-start | bytes 3145728 | tf_op jit(solution)/shard_map/all_to_all | solution.py:296
  12.7 1.3 collective-permute-start.1
  14.1 0.2 collective-permute-start
  14.3 0.1 add_add_fusion
  14.4 0.1 select_reduce_fusion
  14.5 0.0 copy-start.2
  14.5 1.9 %copy-done.2 = bf16[6,1,128,2048]{3,2,1,0:T(8,128)(2,1)S(1)} copy-done((bf16[6,1,128,2048]{3,2,1,0:T(8,128)(2,1)S(1)}, bf16[6,1,128,2048]{3,2,1,0:T(8,128)(2,1)}, u32[]{:S(2)}) %copy-start.2) | copy-done | bytes 3145752
  16.4 1.2 shard_map.113.refs_0_
  17.6 14.0 %collective-permute-done.1.refs_1_ = bf16[16,3,16,512]{3,2,1,0:T(8,128)(2,1)S(1)} collective-permute-done((bf16[16,3,16,512]{3,2,1,0:T(8,128)(2,1)S(1)}, bf16[16,3,16,512]{3,2,1,0:T(8,128)(2,1)S(1)}, u32[]{:S(2)}, u32[]{:S(2)}) %collective-permute-start.1) | collective-permute-done | bytes 786464 | tf_op jit(solution)/shard_map/ppermute | solution.py:307
  31.6 0.4 shard_map.114.refs_2_
  32.0 0.0 copy-start
  32.0 1.1 copy-done
  33.1 16.2 %all-to-all-done.ahead_ref = bf16[16,3,16,1024]{3,2,1,0:T(8,128)(2,1)S(1)} async-done(((bf16[16,3,16,1024]{3,2,1,0:T(8,128)(2,1)}), bf16[16,3,16,1024]{3,2,1,0:T(8,128)(2,1)S(1)}, u32[]{:S(2)}, u32[]{:S(2)}) %all-to-all-start) | async-done | bytes 1572896 | tf_op jit(solution)/shard_map/all_to_all | solution.py:296
  49.3 1.4 copy-done.1
  50.7 2.3 %shard_map.116 = bf16[16,3,16,1024]{3,2,1,0:T(8,128)(2,1)S(1)} custom-call(bf16[16,3,16,1024]{3,2,1,0:T(8,128)(2,1)S(1)} %copy-done.1, bf16[16,3,16,512]{3,2,1,0:T(8,128)(2,1)} %collective-permute-done.refs_1_, bf16[16,3,16,1024]{3,2,1,0:T(8,128)(2,1)S(1)} %shard_map.114.refs_2_, f32[8,128]{1,0:T(8,128)S(1)} %shard_map.115.refs_3_), custom_call_target="tpu_custom_call", output_to_operand_aliasing={{}: (2, {})} | custom-call | flops 393216 | bytes 2359296 | tf_op jit(solution)/shard_map/pallas_call | solution.py:172
  53.0 0.0 copy-start.3
  53.0 0.0 copy-start.8
  53.0 40.7 %all_to_all.15 = bf16[16,3,16,1024]{3,2,1,0:T(8,128)(2,1)S(1)} all-to-all(bf16[16,3,16,1024]{3,2,1,0:T(8,128)(2,1)S(1)} %shard_map.116), channel_id=1, replica_groups=mesh['node'=16,'local'=2] {'node'}, dimensions={0} | all-to-all | bytes 3145728 | tf_op jit(solution)/shard_map/all_to_all | solution.py:296
  93.7 2.7 %shard_map.117 = bf16[16,2,3,16,1024]{4,3,2,1,0:T(8,128)(2,1)S(1)} custom-call(s32[80]{0:T(128)S(1)} %copy-done.7, s32[16]{0:T(128)S(1)} %copy-done.8, s32[96]{0:T(128)S(1)} %compare_select_fusion.refs_5_.new_ref, bf16[48,16,1024]{2,1,0:T(8,128)(2,1)S(1)} %bitcast.2, f32[64,8,1024]{2,1,0:T(8,128)S(1)} %copy-done.3, f32[64,8,1024]{2,1,0:T(8,128)S(1)} %copy-done.4), custom_call_target="tpu_custom_call" | custom-call | flops 5242880 | bytes 8912896 | tf_op jit(solution)/shard_map/pallas_call | solution.py:231
  96.4 74.6 %all_to_all.16.got_ref = bf16[16,2,3,16,1024]{4,3,2,1,0:T(8,128)(2,1)S(1)} all-to-all(bf16[16,2,3,16,1024]{4,3,2,1,0:T(8,128)(2,1)S(1)} %shard_map.117), channel_id=1, replica_groups=mesh['node'=16,'local'=2] {'node'}, dimensions={0} | all-to-all | bytes 6291456 | tf_op jit(solution)/shard_map/all_to_all | solution.py:296
  171.0 4.1 %shard_map.118 = (bf16[6,128,1024]{2,1,0:T(8,128)(2,1)}, f32[6,128,1024]{2,1,0:T(8,128)}, f32[6,128,1024]{2,1,0:T(8,128)}) custom-call(bf16[16,3,16,1024]{3,2,1,0:T(8,128)(2,1)S(1)} %all-to-all-done.ahead_ref, bf16[16,2,3,16,1024]{4,3,2,1,0:T(8,128)(2,1)S(1)} %all_to_all.16.got_ref), custom_call_target="tpu_custom_call" | custom-call | flops 15728640 | bytes 12582912 | tf_op jit(solution)/shard_map/pallas_call | solution.py:274
  (17 shorter events, 0.0 us)
Async XLA Ops:
  6.0 6.7 %copy-start.6 = (bf16[16,3,16,512]{3,2,1,0:T(8,128)(2,1)S(1)}, bf16[16,3,16,512]{3,2,1,0:T(8,128)(2,1)}, u32[]{:S(2)}) copy-start(bf16[16,3,16,512]{3,2,1,0:T(8,128)(2,1)} %get-tuple-element.7.refs_3_) | copy-start | bytes 2359300
  6.0 8.3 %copy-start.9 = (s32[16]{0:T(128)S(1)}, s32[16]{0:T(128)}, u32[]{:S(2)}) copy-start(s32[16]{0:T(128)} %owner_ref.2) | copy-start | bytes 196
  6.0 8.3 %copy-start.10 = (s32[80]{0:T(128)S(1)}, s32[80]{0:T(128)}, u32[]{:S(2)}) copy-start(s32[80]{0:T(128)} %place_ref.2) | copy-start | bytes 964
  6.0 8.4 %copy-start.5 = (bf16[6,1,128,128]{3,2,1,0:T(8,128)(2,1)S(1)}, bf16[6,1,128,128]{3,2,1,0:T(8,128)(2,1)}, u32[]{:S(2)}) copy-start(bf16[6,1,128,128]{3,2,1,0:T(8,128)(2,1)} %refs_1_.1) | copy-start | bytes 589828
  6.0 43.3 %all-to-all-start = ((bf16[16,3,16,1024]{3,2,1,0:T(8,128)(2,1)}), bf16[16,3,16,1024]{3,2,1,0:T(8,128)(2,1)S(1)}, u32[]{:S(2)}, u32[]{:S(2)}) async-start(bf16[16,3,16,1024]{3,2,1,0:T(8,128)(2,1)} %get-tuple-element.6), calls=%async_computation | async-start | bytes 3145728 | tf_op jit(solution)/shard_map/all_to_all | solution.py:296
  12.7 18.8 %collective-permute-start.1 = (bf16[16,3,16,512]{3,2,1,0:T(8,128)(2,1)S(1)}, bf16[16,3,16,512]{3,2,1,0:T(8,128)(2,1)S(1)}, u32[]{:S(2)}, u32[]{:S(2)}) collective-permute-start(bf16[16,3,16,512]{3,2,1,0:T(8,128)(2,1)S(1)} %copy-done.6), channel_id=1, source_target_pairs={{0,1},{1,0},{2,3},{3,2},{4,5},{5,4},{6,7},{7,6},{8,9},{9,8},{10,11... | collective-permute-start | bytes 2359304 | tf_op jit(solution)/shard_map/ppermute | solution.py:307
  14.1 35.3 %collective-permute-start = (bf16[16,3,16,512]{3,2,1,0:T(8,128)(2,1)}, bf16[16,3,16,512]{3,2,1,0:T(8,128)(2,1)}, u32[]{:S(2)}, u32[]{:S(2)}) collective-permute-start(bf16[16,3,16,512]{3,2,1,0:T(8,128)(2,1)} %get-tuple-element.8.refs_4_), channel_id=1, source_target_pairs={{0,1},{1,0},{2,3},{3,2},{4,5},{5,4},{6,7},{7,6},{8,9},{9,8},{10,11... | collective-permute-start | bytes 2359304 | tf_op jit(solution)/shard_map/ppermute | solution.py:307
  14.5 1.9 %copy-start.2 = (bf16[6,1,128,2048]{3,2,1,0:T(8,128)(2,1)S(1)}, bf16[6,1,128,2048]{3,2,1,0:T(8,128)(2,1)}, u32[]{:S(2)}) copy-start(bf16[6,1,128,2048]{3,2,1,0:T(8,128)(2,1)} %refs_2_.1) | copy-start | bytes 9437188
  32.0 1.1 copy-start
  49.3 1.4 copy-start.1
  50.7 43.0 %copy-start.4 = (f32[64,8,1024]{2,1,0:T(8,128)S(1)}, f32[64,8,1024]{2,1,0:T(8,128)}, u32[]{:S(2)}) copy-start(f32[64,8,1024]{2,1,0:T(8,128)} %second_ref.1) | copy-start | bytes 6291460
  53.0 40.7 %copy-start.3 = (f32[64,8,1024]{2,1,0:T(8,128)S(1)}, f32[64,8,1024]{2,1,0:T(8,128)}, u32[]{:S(2)}) copy-start(f32[64,8,1024]{2,1,0:T(8,128)} %first_ref.1) | copy-start | bytes 6291460
  53.0 40.7 %copy-start.7 = (s32[80]{0:T(128)S(1)}, s32[80]{0:T(128)}, u32[]{:S(2)}) copy-start(s32[80]{0:T(128)} %place_ref.3) | copy-start | bytes 964
  53.0 40.7 %copy-start.8 = (s32[16]{0:T(128)S(1)}, s32[16]{0:T(128)}, u32[]{:S(2)}) copy-start(s32[16]{0:T(128)} %owner_ref.3) | copy-start | bytes 196

commit v4 on v3

--- a/solution.py
+++ b/solution.py
@@ -86,11 +86,12 @@
     pairs = capacity // 2
     shape = jax.ShapeDtypeStruct((nodes, pairs, 2 * rows // nodes, columns), jnp.bfloat16)
     block = pl.BlockSpec((nodes, 1) + shape.shape[2:], lambda i, *_: (0, i, 0, 0))
-    part = jax.ShapeDtypeStruct(shape.shape[:3] + (columns // 2,), jnp.bfloat16)
-    part_block = pl.BlockSpec((nodes, 1) + part.shape[2:], lambda i, *_: (0, i, 0, 0))
+    widths = (columns * 7 // 8, columns // 8)
+    parts = [jax.ShapeDtypeStruct(shape.shape[:3] + (width,), jnp.bfloat16) for width in widths]
+    part_blocks = [pl.BlockSpec((nodes, 1) + part.shape[2:], lambda i, *_: (0, i, 0, 0)) for part in parts]
     return pl.pallas_call(
         front_kernel,
-        out_shape=[shape, part, part],
+        out_shape=[shape, *parts],
         grid_spec=pltpu.PrefetchScalarGridSpec(
             num_scalar_prefetch=3,
             grid=(pairs,),
@@ -99,7 +100,7 @@
                 pl.BlockSpec((2, 1, tokens, columns), lambda i, s, *_: (i, 0, 0, 1 - s[0])),
                 pl.BlockSpec(weight.shape, lambda i, *_: (0, 0, 0)),
             ],
-            out_specs=[block, part_block, part_block],
+            out_specs=[block, *part_blocks],
             scratch_shapes=[pltpu.SMEM((nodes * capacity,), jnp.int32)],
         ),
         compiler_params=pltpu.CompilerParams(vmem_limit_bytes=VMEM_LIMIT),
@@ -306,7 +307,7 @@
     ours = gradient_call(nodes, side, features, grad_out, (*theirs, new_table))
     low, high = (lax.ppermute(part, "local", [(0, 1), (1, 0)]) for part in theirs)
     blocks = add_call(0, ours, low)
-    blocks = exchange(add_call(1, ours, high, (blocks,), (arrived_call(ahead),)))
+    blocks = exchange(add_call(7, ours, high, (blocks,), (arrived_call(ahead),)))
     send = update_call(blocks, old_place, old_owner, new_table, first_moment, second_moment)
     return tuple(place_call(ahead, exchange(send)))
 
@@ -356,7 +357,7 @@
         and capacity % 2 == 0
         and rows % 8 == 0
         and experts % 4 == 0
-        and columns % 256 == 0
+        and columns % 1024 == 0
     ):
         return paired(*state, old_place, new_place, old_owner, new_owner, new_table)
     old_table = position_table(old_place, jnp.concatenate([primaries, old_owner]), positions, experts)

time: 177 us -> 175 us (0.989)
  Pallas kernels: 16.1 us -> 14.3 us
    all_to_all x1, waiting for transfers between devices: 16.2 us -> 3.12 us  [exchange(): lax.all_to_all(array, 'node', split_axis=0, concat_axis=0, tiled=True)]
    ppermute x2, waiting for transfers between devices: 14 us -> 26.6 us  [paired(): lax.ppermute(part, 'local', [(0, 1), (1, 0)])]
    unnamed x22 -> x24, local copies, waits for them, and re-layouts: 4.47 us -> 4.47 us
where the time goes in v4:
time: 175 us; the launch traced here: 173 us
  blocking collectives  115 us (66%)
  waiting for transfers between devices  29.7 us (17%)
  Pallas kernels  14.3 us (8%)
  starting transfers between devices  8.23 us (5%)
  local copies, waits for them, and re-layouts  4.48 us (3%)
    all_to_all x2, blocking collectives, exchange(): lax.all_to_all(array, 'node', split_axis=0, concat_axis=0, tiled=True)  115 us
    ppermute x2, waiting for transfers between devices, paired(): lax.ppermute(part, 'local', [(0, 1), (1, 0)])  26.6 us
    all_to_all x1, starting transfers between devices, exchange(): lax.all_to_all(array, 'node', split_axis=0, concat_axis=0, tiled=True)  6.7 us
    pallas_call x1, Pallas kernels, front_call(): pl.pallas_call(front_kernel, out_shape=[shape, *parts], grid_spec=pltpu.P...  5.37 us
    unnamed x24, local copies, waits for them, and re-layouts  4.47 us
    pallas_call x1, Pallas kernels, place_call(): pl.pallas_call(place_kernel, out_shape=[jax.ShapeDtypeStruct((2 * pairs,...  4.09 us
  transfers between devices with their start and end apart: 3, of which 2 were waited for; matrix products, arithmetic and copies ran while one was open for 0% of the time, Pallas kernels for 1%

profile of v4, /device:TPU:11, one launch (start us, length us, event | category | flops | bytes accessed | tf_op | source)
XLA Modules:
  0.0 173.1 jit_solution(2037851524122349320)
XLA Ops:
  0.6 5.4 %shard_map.112 = (bf16[16,3,16,1024]{3,2,1,0:T(8,128)(2,1)}, bf16[16,3,16,896]{3,2,1,0:T(8,128)(2,1)}, bf16[16,3,16,128]{3,2,1,0:T(8,128)(2,1)}) custom-call(s32[1]{0:T(128)} %bitcast.side_ref.refs_0_, s32[80]{0:T(128)} %place_ref.2, s32[16]{0:T(128)} %owner_ref.2, bf16[6,1,128,128]{3,2,1,0:T(8,128)(2,1)} %refs_1_.1, bf16[6,1,128,2048]{3,2,1,0:T(8,128)(2,1)} %refs_2_.1, ...), custom_call_target="tpu_custom_call" | custom-call | flops 201326592 | bytes 6291456 | tf_op jit(solution)/shard_map/pallas_call | solution.py:92
  6.0 0.0 copy-start.11
  6.0 0.0 copy-start.6
  6.0 6.7 %all-to-all-start = ((bf16[16,3,16,1024]{3,2,1,0:T(8,128)(2,1)}), bf16[16,3,16,1024]{3,2,1,0:T(8,128)(2,1)S(1)}, u32[]{:S(2)}, u32[]{:S(2)}) async-start(bf16[16,3,16,1024]{3,2,1,0:T(8,128)(2,1)} %get-tuple-element.6), calls=%async_computation | async-start | bytes 3145728 | tf_op jit(solution)/shard_map/all_to_all | solution.py:297
  12.8 1.3 collective-permute-start.1
  14.1 0.2 collective-permute-start
  14.3 0.1 add_add_fusion
  14.4 0.1 select_reduce_fusion
  14.5 0.0 copy-start.2
  14.5 1.9 %copy-done.2 = bf16[6,1,128,2048]{3,2,1,0:T(8,128)(2,1)S(1)} copy-done((bf16[6,1,128,2048]{3,2,1,0:T(8,128)(2,1)S(1)}, bf16[6,1,128,2048]{3,2,1,0:T(8,128)(2,1)}, u32[]{:S(2)}) %copy-start.2) | copy-done | bytes 3145752
  16.4 1.2 shard_map.113.refs_0_
  17.6 26.6 %collective-permute-done.1.refs_1_ = bf16[16,3,16,896]{3,2,1,0:T(8,128)(2,1)S(1)} collective-permute-done((bf16[16,3,16,896]{3,2,1,0:T(8,128)(2,1)S(1)}, bf16[16,3,16,896]{3,2,1,0:T(8,128)(2,1)S(1)}, u32[]{:S(2)}, u32[]{:S(2)}) %collective-permute-start.1) | collective-permute-done | bytes 1376288 | tf_op jit(solution)/shard_map/ppermute | solution.py:308
  44.2 0.7 shard_map.114.refs_2_
  45.0 0.0 copy-start
  45.0 1.1 copy-done
  46.1 3.1 %all-to-all-done.ahead_ref = bf16[16,3,16,1024]{3,2,1,0:T(8,128)(2,1)S(1)} async-done(((bf16[16,3,16,1024]{3,2,1,0:T(8,128)(2,1)}), bf16[16,3,16,1024]{3,2,1,0:T(8,128)(2,1)S(1)}, u32[]{:S(2)}, u32[]{:S(2)}) %all-to-all-start) | async-done | bytes 1572896 | tf_op jit(solution)/shard_map/all_to_all | solution.py:297
  49.2 1.4 copy-done.1
  50.6 0.2 shard_map.116
  50.9 0.0 copy-start.3
  50.9 0.0 copy-start.8
  50.9 40.8 %all_to_all.15 = bf16[16,3,16,1024]{3,2,1,0:T(8,128)(2,1)S(1)} all-to-all(bf16[16,3,16,1024]{3,2,1,0:T(8,128)(2,1)S(1)} %shard_map.116), channel_id=1, replica_groups=mesh['node'=16,'local'=2] {'node'}, dimensions={0} | all-to-all | bytes 3145728 | tf_op jit(solution)/shard_map/all_to_all | solution.py:297
  91.7 2.7 %shard_map.117 = bf16[16,2,3,16,1024]{4,3,2,1,0:T(8,128)(2,1)S(1)} custom-call(s32[80]{0:T(128)S(1)} %copy-done.8, s32[16]{0:T(128)S(1)} %copy-done.9, s32[96]{0:T(128)S(1)} %compare_select_fusion.refs_5_.new_ref, bf16[48,16,1024]{2,1,0:T(8,128)(2,1)S(1)} %bitcast.2, f32[64,8,1024]{2,1,0:T(8,128)S(1)} %copy-done.3, f32[64,8,1024]{2,1,0:T(8,128)S(1)} %copy-done.4), custom_call_target="tpu_custom_call" | custom-call | flops 5242880 | bytes 8912896 | tf_op jit(solution)/shard_map/pallas_call | solution.py:232
  94.4 74.6 %all_to_all.16.got_ref = bf16[16,2,3,16,1024]{4,3,2,1,0:T(8,128)(2,1)S(1)} all-to-all(bf16[16,2,3,16,1024]{4,3,2,1,0:T(8,128)(2,1)S(1)} %shard_map.117), channel_id=1, replica_groups=mesh['node'=16,'local'=2] {'node'}, dimensions={0} | all-to-all | bytes 6291456 | tf_op jit(solution)/shard_map/all_to_all | solution.py:297
  169.0 4.1 %shard_map.118 = (bf16[6,128,1024]{2,1,0:T(8,128)(2,1)}, f32[6,128,1024]{2,1,0:T(8,128)}, f32[6,128,1024]{2,1,0:T(8,128)}) custom-call(bf16[16,3,16,1024]{3,2,1,0:T(8,128)(2,1)S(1)} %all-to-all-done.ahead_ref, bf16[16,2,3,16,1024]{4,3,2,1,0:T(8,128)(2,1)S(1)} %all_to_all.16.got_ref), custom_call_target="tpu_custom_call" | custom-call | flops 15728640 | bytes 12582912 | tf_op jit(solution)/shard_map/pallas_call | solution.py:275
  (19 shorter events, 0.0 us)
Async XLA Ops:
  6.0 6.7 %copy-start.5 = (bf16[16,3,16,896]{3,2,1,0:T(8,128)(2,1)S(1)}, bf16[16,3,16,896]{3,2,1,0:T(8,128)(2,1)}, u32[]{:S(2)}) copy-start(bf16[16,3,16,896]{3,2,1,0:T(8,128)(2,1)} %get-tuple-element.7.refs_3_) | copy-start | bytes 4128772
  6.0 8.1 %copy-start.7 = (bf16[16,3,16,128]{3,2,1,0:T(8,128)(2,1)S(1)}, bf16[16,3,16,128]{3,2,1,0:T(8,128)(2,1)}, u32[]{:S(2)}) copy-start(bf16[16,3,16,128]{3,2,1,0:T(8,128)(2,1)} %get-tuple-element.8.refs_4_) | copy-start | bytes 589828
  6.0 8.3 %copy-start.10 = (s32[16]{0:T(128)S(1)}, s32[16]{0:T(128)}, u32[]{:S(2)}) copy-start(s32[16]{0:T(128)} %owner_ref.2) | copy-start | bytes 196
  6.0 8.3 %copy-start.11 = (s32[80]{0:T(128)S(1)}, s32[80]{0:T(128)}, u32[]{:S(2)}) copy-start(s32[80]{0:T(128)} %place_ref.2) | copy-start | bytes 964
  6.0 8.5 %copy-start.6 = (bf16[6,1,128,128]{3,2,1,0:T(8,128)(2,1)S(1)}, bf16[6,1,128,128]{3,2,1,0:T(8,128)(2,1)}, u32[]{:S(2)}) copy-start(bf16[6,1,128,128]{3,2,1,0:T(8,128)(2,1)} %refs_1_.1) | copy-start | bytes 589828
  6.0 43.2 %all-to-all-start = ((bf16[16,3,16,1024]{3,2,1,0:T(8,128)(2,1)}), bf16[16,3,16,1024]{3,2,1,0:T(8,128)(2,1)S(1)}, u32[]{:S(2)}, u32[]{:S(2)}) async-start(bf16[16,3,16,1024]{3,2,1,0:T(8,128)(2,1)} %get-tuple-element.6), calls=%async_computation | async-start | bytes 3145728 | tf_op jit(solution)/shard_map/all_to_all | solution.py:297
  12.8 31.5 %collective-permute-start.1 = (bf16[16,3,16,896]{3,2,1,0:T(8,128)(2,1)S(1)}, bf16[16,3,16,896]{3,2,1,0:T(8,128)(2,1)S(1)}, u32[]{:S(2)}, u32[]{:S(2)}) collective-permute-start(bf16[16,3,16,896]{3,2,1,0:T(8,128)(2,1)S(1)} %copy-done.5), channel_id=1, source_target_pairs={{0,1},{1,0},{2,3},{3,2},{4,5},{5,4},{6,7},{7,6},{8,9},{9,8},{10,11... | collective-permute-start | bytes 4128776 | tf_op jit(solution)/shard_map/ppermute | solution.py:308
  14.1 35.2 %collective-permute-start = (bf16[16,3,16,128]{3,2,1,0:T(8,128)(2,1)S(1)}, bf16[16,3,16,128]{3,2,1,0:T(8,128)(2,1)S(1)}, u32[]{:S(2)}, u32[]{:S(2)}) collective-permute-start(bf16[16,3,16,128]{3,2,1,0:T(8,128)(2,1)S(1)} %copy-done.7), channel_id=1, source_target_pairs={{0,1},{1,0},{2,3},{3,2},{4,5},{5,4},{6,7},{7,6},{8,9},{9,8},{10,11... | collective-permute-start | bytes 589832 | tf_op jit(solution)/shard_map/ppermute | solution.py:308
  14.5 1.9 %copy-start.2 = (bf16[6,1,128,2048]{3,2,1,0:T(8,128)(2,1)S(1)}, bf16[6,1,128,2048]{3,2,1,0:T(8,128)(2,1)}, u32[]{:S(2)}) copy-start(bf16[6,1,128,2048]{3,2,1,0:T(8,128)(2,1)} %refs_2_.1) | copy-start | bytes 9437188
  45.0 1.1 copy-start
  49.2 1.4 copy-start.1
  50.6 41.0 %copy-start.4 = (f32[64,8,1024]{2,1,0:T(8,128)S(1)}, f32[64,8,1024]{2,1,0:T(8,128)}, u32[]{:S(2)}) copy-start(f32[64,8,1024]{2,1,0:T(8,128)} %second_ref.1) | copy-start | bytes 6291460
  50.9 40.8 %copy-start.3 = (f32[64,8,1024]{2,1,0:T(8,128)S(1)}, f32[64,8,1024]{2,1,0:T(8,128)}, u32[]{:S(2)}) copy-start(f32[64,8,1024]{2,1,0:T(8,128)} %first_ref.1) | copy-start | bytes 6291460
  50.9 40.8 %copy-start.8 = (s32[80]{0:T(128)S(1)}, s32[80]{0:T(128)}, u32[]{:S(2)}) copy-start(s32[80]{0:T(128)} %place_ref.3) | copy-start | bytes 964
  50.9 40.8 %copy-start.9 = (s32[16]{0:T(128)S(1)}, s32[16]{0:T(128)}, u32[]{:S(2)}) copy-start(s32[16]{0:T(128)} %owner_ref.3) | copy-start | bytes 196
